TPU v7x, 128 devices: a whole 4x4x4 slice. The times are simulated.
128 devices in a mesh: echo: 8 (over x, core), plane: 16 (over z, y).
Axes of the slice: x: 4, y: 4, z: 4, core: 2. Of those that a mesh axis runs over, the one named last changes fastest.
Arguments:
- acquired: bfloat16 [8, 8, 16, 256, 1024], P('echo', None, 'plane'), may hold values from -3 to 3
- coil_maps: bfloat16 [8, 16, 256, 1024], P(None, 'plane'), may hold values from -2.09375 to 2.09375
- mask_words: int32 [8, 256, 18], P('echo'), may hold values from 0 to 1073741823, as said below
- start_image: float32 [8, 16, 256, 1024], P('echo', 'plane'), may hold values from -36 to 36
Outputs:
- solved_image: float32 [8, 16, 256, 1024], P('echo', 'plane')
Inputs may be any that keep to these rules, and one draw needn't show every extreme that they name: Bit j of mask_words[e, z, w] is 1 where echo e samples ky = 30 w + j at kz = z; bits for ky at or above 512 are 0.
All inputs are finite; a program needn't handle non-finite values.
Results may differ from a plain program's by a relative error of at most 0.0009.
Values sent between devices are 32-bit elements; how exact they have to be, the bound alone decides.
A program may use at most 192 MiB of HBM per device.

v0:
```python
import math

import jax
import jax.numpy as jnp
from jax import lax
from jax.sharding import PartitionSpec as P

NY = 512
NZ = 256
ITERS = 2


DUAL_STEP = 0.25
PRIMAL_STEP = 0.25
RADIUS_FACTOR = 0.5
EPSILON = 1e-06


def passed_along(value, axis, by):
    peers = lax.axis_size(axis)
    pairs = [(i, i + by) for i in range(peers) if 0 <= i + by < peers]
    return lax.ppermute(value, axis, pairs)


def make_tables(count):
    index = jnp.arange(count, dtype=jnp.int32)
    angle = (index[:, None] * index[None, :] % count).astype(jnp.float32) * (2.0 * math.pi / count)
    scale = 1.0 / math.sqrt(count)
    return (
        (jnp.cos(angle) * scale).astype(jnp.bfloat16),
        (jnp.sin(angle) * scale).astype(jnp.bfloat16),
    )


def ky_kernel(cosine, sine, forward):
    if forward:
        upper = jnp.concatenate([cosine, -sine], 1)
        lower = jnp.concatenate([sine, cosine], 1)
    else:
        upper = jnp.concatenate([cosine, sine], 1)
        lower = jnp.concatenate([-sine, cosine], 1)
    return jnp.concatenate([upper, lower], 0)


def along_kz(half, cosine, sine, forward, width):
    first = jnp.einsum("zw,bwk->bzk", cosine, half, preferred_element_type=jnp.float32)
    second = jnp.einsum("zw,bwk->bzk", sine, half, preferred_element_type=jnp.float32)
    if forward:
        real_part = first[..., :width] + second[..., width:]
        imaginary = first[..., width:] - second[..., :width]
    else:
        real_part = first[..., :width] - second[..., width:]
        imaginary = first[..., width:] + second[..., :width]
    return jnp.concatenate([real_part, imaginary], -1)


def times_maps(maps, field, width, conjugate):
    map_real = maps[..., :width].astype(jnp.float32)
    map_imaginary = maps[..., width:].astype(jnp.float32)
    field_real = field[..., :width]
    field_imaginary = field[..., width:]
    if conjugate:
        real_part = map_real * field_real + map_imaginary * field_imaginary
        imaginary = map_real * field_imaginary - map_imaginary * field_real
    else:
        real_part = map_real * field_real - map_imaginary * field_imaginary
        imaginary = map_real * field_imaginary + map_imaginary * field_real
    return jnp.concatenate([real_part, imaginary], -1)


def unpack_mask(words, width):
    spread = jnp.repeat(words, 30, axis=-1)[..., :width]
    offset = jnp.arange(width, dtype=jnp.int32) % 30
    sampled = (jnp.right_shift(spread, offset) % 2).astype(jnp.float32)
    return jnp.concatenate([sampled, sampled], -1)


def forward_model(image, maps, kernel, cosine, sine, width):
    coil = times_maps(maps[None], image[:, None], width, False).astype(jnp.bfloat16)
    shape = coil.shape
    half = jnp.dot(coil.reshape(-1, 2 * width), kernel, preferred_element_type=jnp.float32).astype(
        jnp.bfloat16
    )
    half = half.reshape(-1, shape[-2], 2 * width)
    return along_kz(half, cosine, sine, True, width).reshape(shape)


def adjoint_model(dual, maps, kernel, cosine, sine, width):
    shape = dual.shape
    flat = dual.astype(jnp.bfloat16).reshape(-1, shape[-2], 2 * width)
    half = along_kz(flat, cosine, sine, False, width).astype(jnp.bfloat16)
    spatial = jnp.dot(
        half.reshape(-1, 2 * width), kernel, preferred_element_type=jnp.float32
    ).reshape(shape)
    return jnp.sum(times_maps(maps[None], spatial, width, True), axis=1)


def inner_gradients(field, width):
    grad_z = jnp.concatenate(
        [field[:, :, 1:] - field[:, :, :-1], jnp.zeros_like(field[:, :, :1])], 2
    )
    diff_y = jnp.concatenate([field[..., 1:] - field[..., :-1], jnp.zeros_like(field[..., :1])], 3)
    keep_y = jnp.arange(2 * width, dtype=jnp.int32) % width < width - 1
    return (grad_z, jnp.where(keep_y, diff_y, 0.0))


def inner_transpose(dual_z, dual_y):
    part_z = jnp.concatenate([jnp.zeros_like(dual_z[:, :, :1]), dual_z[:, :, :-1]], 2) - dual_z
    part_y = jnp.concatenate([jnp.zeros_like(dual_y[..., :1]), dual_y[..., :-1]], 3) - dual_y
    return part_z + part_y


def shards(acquired, coil_maps, mask_words, start_image):
    width = NY
    planes = start_image.shape[1]
    first = lax.axis_index("plane") * planes
    span = lax.axis_size("plane") * planes
    count = lax.axis_size("echo") * start_image.shape[0] * span * NZ * NY
    cos_y, sin_y = make_tables(NY)
    cos_z, sin_z = make_tables(NZ)
    kernel_forward = ky_kernel(cos_y, sin_y, True)
    kernel_inverse = ky_kernel(cos_y, sin_y, False)
    sampled = unpack_mask(mask_words, width)
    power_local = jnp.sum(start_image * start_image)
    power = lax.psum(power_local, ("echo", "plane"))
    radius = RADIUS_FACTOR * jnp.sqrt(power / count + EPSILON)
    dual_shape = (start_image.shape[0], planes) + start_image.shape[2:]
    dual_x = jnp.zeros(dual_shape, jnp.float32)
    dual_z = jnp.zeros(dual_shape, jnp.float32)
    dual_y = jnp.zeros(dual_shape, jnp.float32)
    dual_data = jnp.zeros(acquired.shape, jnp.float32)
    current = start_image
    extra = start_image
    for step in range(ITERS):
        above = passed_along(extra, "plane", -1)
        grad_x = jnp.concatenate([extra[:, 1:], above], 1) - extra
        position = first + jnp.arange(planes, dtype=jnp.int32)
        grad_x = jnp.where((position < span - 1)[None, :, None, None], grad_x, 0.0)
        grad_z, grad_y = inner_gradients(extra, width)
        spectra = forward_model(extra, coil_maps, kernel_forward, cos_z, sin_z, width)
        dual_x = dual_x + DUAL_STEP * grad_x
        dual_z = dual_z + DUAL_STEP * grad_z
        dual_y = dual_y + DUAL_STEP * grad_y
        squares = jnp.sum(dual_x * dual_x + dual_z * dual_z + dual_y * dual_y, axis=0)
        squares = squares[..., :width] + squares[..., width:]
        total = lax.psum(squares, "echo")
        shrink = 1.0 / jnp.maximum(1.0, jnp.sqrt(total) / radius)
        shrink = jnp.concatenate([shrink, shrink], -1)[None]
        dual_x = dual_x * shrink
        dual_z = dual_z * shrink
        dual_y = dual_y * shrink
        residual = spectra - acquired.astype(jnp.float32)
        dual_data = (dual_data + DUAL_STEP * sampled[:, None, None] * residual) / (1.0 + DUAL_STEP)
        back = adjoint_model(dual_data, coil_maps, kernel_inverse, cos_z, sin_z, width)
        below = passed_along(dual_x, "plane", 1)
        part_x = jnp.concatenate([below, dual_x[:, :-1]], 1) - dual_x
        transposed = part_x + inner_transpose(dual_z, dual_y)
        updated = current - PRIMAL_STEP * (back + transposed)
        extra = 2.0 * updated - current
        current = updated
    return current


def solution(mesh):
    in_specs = (
        P("echo", None, "plane", None, None),
        P(None, "plane", None, None),
        P("echo", None, None),
        P("echo", "plane", None, None),
    )
    out_specs = P("echo", "plane", None, None)
    return jax.shard_map(shards, mesh=mesh, in_specs=in_specs, out_specs=out_specs, check_vma=False)
```

profile of v0, /device:TPU:32, one launch (start us, length us, event | category | flops | bytes accessed | tf_op | source)
XLA Modules:
  0.0 345.0 jit_solution(1656422578618875802)
XLA Ops:
  6.5 4.6 %collective-permute-start = (f32[1,1,256,1024]{3,2,1,0:T(8,128)}, f32[1,1,256,1024]{3,2,1,0:T(8,128)}, u32[]{:S(2)}, u32[]{:S(2)}) collective-permute-start(f32[1,1,256,1024]{3,2,1,0:T(8,128)} %param.7), channel_id=1, source_target_pairs={{1,0},{2,1},{3,2},{4,3},{5,4},{6,5},{7,6},{8,7},{9,8},{10,9},{11,1... | collective-permute-start | bytes 3145736 | tf_op jit(solution)/shard_map/ppermute | solution.py:22
  11.2 4.0 %fusion.94 = bf16[512,512]{1,0:T(8,128)(2,1)S(1)} fusion(), kind=kLoop, calls=%fused_computation.159 | loop fusion | flops 4980736 | bytes 524288 | tf_op jit(solution)/shard_map/neg | solution.py:37
  15.2 1.9 slice_subtract_fusion.7
  17.1 1.3 slice_subtract_fusion.6
  18.5 4.6 %multiply_convert_fusion = (bf16[512,512]{1,0:T(8,128)(2,1)S(1)}, bf16[512,512]{1,0:T(8,128)(2,1)S(1)}) fusion(), kind=kLoop, calls=%fused_computation.129 | loop fusion | flops 4718592 | bytes 1048576 | tf_op jit(solution)/shard_map/convert_element_type | solution.py:31
  23.1 1.5 fusion.9
  24.6 4.5 %fusion.47 = bf16[2048,1024]{1,0:T(8,128)(2,1)S(1)} fusion(bf16[2048,512]{1,0:T(8,128)(2,1)S(1)} %bitcast.143, bf16[2048,512]{1,0:T(8,128)(2,1)S(1)} %bitcast.142, bf16[512,512]{1,0:T(8,128)(2,1)S(1)} %get-tuple-element.38, bf16[512,512]{1,0:T(8,128)(2,1)S(1)} %get-tuple-element.37, bf16[512,512]{1,0:T(8,128)(2,1)S(1)} %fusion.94), kind=kOutput, calls=%fused_computation.75 | convolution fusion | flops 4313841664 | bytes 9961472 | tf_op jit(solution)/shard_map/dot_general | solution.py:81
  29.2 5.5 %convolution_bitcast_fusion.4 = f32[8,256,1024]{1,2,0:T(8,128)} fusion(bf16[8,256,1024]{2,1,0:T(8,128)(2,1)S(1)} %bitcast.134), kind=kOutput, calls=%fused_computation.84 | convolution fusion | flops 1074790400 | bytes 12582912 | tf_op jit(solution)/shard_map/zw,bwk->bzk/dot_general | solution.py:47
  34.7 5.5 %convolution_bitcast_fusion.5 = f32[8,256,1024]{1,2,0:T(8,128)} fusion(bf16[8,256,1024]{2,1,0:T(8,128)(2,1)S(1)} %bitcast.135), kind=kOutput, calls=%fused_computation.85 | convolution fusion | flops 1074790400 | bytes 12582912 | tf_op jit(solution)/shard_map/zw,bwk->bzk/dot_general | solution.py:46
  41.1 1.3 fusion.87
  42.4 1.1 fusion.70
  43.5 6.5 %copy.14 = bf16[1,8,1,256,1024]{3,4,1,2,0:T(8,128)(2,1)} copy(bf16[1,8,1,256,1024]{4,3,2,1,0:T(8,128)(2,1)} %param.4) | data formatting | bytes 8388608 | tf_op args[0]
  50.0 10.5 %slice_add_fusion.3 = (f32[8,256,512]{1,2,0:T(8,128)}, f32[8,256,512]{1,2,0:T(8,128)}) fusion(f32[8,256,1024]{1,2,0:T(8,128)} %convolution_bitcast_fusion.4, f32[8,256,1024]{1,2,0:T(8,128)} %convolution_bitcast_fusion.5), kind=kLoop, calls=%fused_computation.53 | loop fusion | flops 2097152 | bytes 25165824 | tf_op jit(solution)/shard_map/add | solution.py:49
  60.5 4.7 %fusion.7 = bf16[8,256,1024]{1,2,0:T(8,128)(2,1)S(1)} fusion(bf16[1,8,1,256,1024]{3,4,1,2,0:T(8,128)(2,1)S(1)} %copy-done.4, f32[8,256,512]{1,2,0:T(8,128)} %get-tuple-element.16, f32[8,256,512]{1,2,0:T(8,128)} %get-tuple-element.15, f32[256,1024]{0,1:T(8,128)} %fusion.70), kind=kLoop, calls=%fused_computation.29 | loop fusion | flops 12582912 | bytes 17825792 | tf_op jit(solution)/shard_map/reshape | solution.py:90
  65.2 5.5 %convolution_bitcast_fusion.2 = f32[8,256,1024]{1,2,0:T(8,128)} fusion(bf16[8,256,1024]{1,2,0:T(8,128)(2,1)S(1)} %fusion.7), kind=kOutput, calls=%fused_computation.82 | convolution fusion | flops 1074790400 | bytes 12582912 | tf_op jit(solution)/shard_map/zw,bwk->bzk/dot_general | solution.py:47
  70.7 5.5 %convolution_bitcast_fusion.3 = f32[8,256,1024]{1,2,0:T(8,128)} fusion(bf16[8,256,1024]{1,2,0:T(8,128)(2,1)S(1)} %fusion.7), kind=kOutput, calls=%fused_computation.83 | convolution fusion | flops 1074790400 | bytes 12582912 | tf_op jit(solution)/shard_map/zw,bwk->bzk/dot_general | solution.py:46
  76.2 2.4 multiply_reduce_fusion
  79.5 8.6 %fusion.23 = (bf16[8,256,512]{1,2,0:T(8,128)(2,1)}, bf16[8,256,512]{1,2,0:T(8,128)(2,1)}) fusion(f32[8,256,1024]{1,2,0:T(8,128)} %convolution_bitcast_fusion.2, f32[8,256,1024]{1,2,0:T(8,128)} %convolution_bitcast_fusion.3), kind=kLoop, calls=%fused_computation.51 | loop fusion | flops 4194304 | bytes 20971520 | tf_op jit(solution)/shard_map/convert.6
  88.1 65.6 %psum.22 = f32[]{:T(128)} all-reduce(f32[]{:T(128)} %get-tuple-element.29), channel_id=1, replica_groups=mesh['echo'=8,'plane'=16] {'echo','plane'}, use_global_device_ids=true, to_apply=%region_3.4 | all-reduce | flops 1 | bytes 8 | tf_op jit(solution)/shard_map/psum | solution.py:125
  154.5 1.2 maximum_divide_fusion.1
  155.7 2.3 fusion.73
  158.1 2.8 collective-permute-start.1
  160.9 4.6 %fusion.53 = f32[1,8,1,256,1024]{4,3,1,2,0:T(8,128)S(1)} fusion(bf16[8,256,512]{1,2,0:T(8,128)(2,1)S(1)} %copy-done.18, bf16[8,256,512]{1,2,0:T(8,128)(2,1)S(1)} %copy-done.17, bf16[512,512]{1,0:T(8,128)(2,1)S(1)} %copy-done.30, bf16[512,512]{1,0:T(8,128)(2,1)S(1)} %copy-done.22, bf16[512,512]{1,0:T(8,128)(2,1)S(1)} %copy-done.26), kind=kOutput, calls=%fused_computation.77 | convolution fusion | flops 4311744512 | bytes 14155776 | tf_op jit(solution)/shard_map/dot_general | solution.py:92
  165.6 1.7 fusion.12
  168.3 18.7 %collective-permute-done.1 = f32[1,1,256,1024]{3,2,1,0:T(8,128)S(1)} collective-permute-done((f32[1,1,256,1024]{3,2,1,0:T(8,128)S(1)}, f32[1,1,256,1024]{3,2,1,0:T(8,128)S(1)}, u32[]{:S(2)}, u32[]{:S(2)}) %collective-permute-start.1) | collective-permute-done | bytes 1048608 | tf_op jit(solution)/shard_map/ppermute | solution.py:22
  187.0 1.9 multiply_subtract_fusion
  189.0 1.1 slice_subtract_fusion.5
  190.1 1.3 slice_subtract_fusion.4
  191.4 2.6 collective-permute-start.2
  194.1 1.4 fusion.15
  195.5 4.5 %fusion.44 = bf16[2048,1024]{1,0:T(8,128)(2,1)S(1)} fusion(bf16[2048,512]{1,0:T(8,128)(2,1)S(1)} %bitcast.145, bf16[2048,512]{1,0:T(8,128)(2,1)S(1)} %bitcast.144, bf16[512,512]{1,0:T(8,128)(2,1)S(1)} %copy-done.31, bf16[512,512]{1,0:T(8,128)(2,1)S(1)} %copy-done.27, bf16[512,512]{1,0:T(8,128)(2,1)S(1)} %copy-done.23), kind=kOutput, calls=%fused_computation.74 | convolution fusion | flops 4313841664 | bytes 9961472 | tf_op jit(solution)/shard_map/dot_general | solution.py:81
  200.0 5.5 %convolution_bitcast_fusion = f32[8,256,1024]{1,2,0:T(8,128)} fusion(bf16[8,256,1024]{2,1,0:T(8,128)(2,1)S(1)} %bitcast.136), kind=kOutput, calls=%fused_computation.80 | convolution fusion | flops 1074790400 | bytes 12582912 | tf_op jit(solution)/shard_map/zw,bwk->bzk/dot_general | solution.py:47
  205.6 5.5 %convolution_bitcast_fusion.1 = f32[8,256,1024]{1,2,0:T(8,128)} fusion(bf16[8,256,1024]{2,1,0:T(8,128)(2,1)S(1)} %bitcast.137), kind=kOutput, calls=%fused_computation.81 | convolution fusion | flops 1074790400 | bytes 12582912 | tf_op jit(solution)/shard_map/zw,bwk->bzk/dot_general | solution.py:46
  211.1 10.6 %slice_add_fusion.1 = (f32[8,256,512]{1,2,0:T(8,128)}, f32[8,256,512]{1,2,0:T(8,128)}) fusion(f32[8,256,1024]{1,2,0:T(8,128)} %convolution_bitcast_fusion, f32[8,256,1024]{1,2,0:T(8,128)} %convolution_bitcast_fusion.1), kind=kLoop, calls=%fused_computation.47 | loop fusion | flops 2097152 | bytes 25165824 | tf_op jit(solution)/shard_map/add | solution.py:49
  221.6 7.5 %fusion.5 = bf16[1,8,1,256,1024]{3,4,1,2,0:T(8,128)(2,1)S(1)} fusion(bf16[1,8,1,256,1024]{3,4,1,2,0:T(8,128)(2,1)S(1)} %copy-done.5, f32[8,256,512]{1,2,0:T(8,128)} %get-tuple-element.12, f32[8,256,512]{1,2,0:T(8,128)} %get-tuple-element.11, f32[8,256,512]{1,2,0:T(8,128)} %get-tuple-element.16, f32[8,256,512]{1,2,0:T(8,128)} %get-tuple-element.15, ...), kind=kLoop, calls=%fused_computation.23 | loop fusion | flops 23068672 | bytes 26214400 | tf_op jit(solution)/shard_map/convert_element_type | solution.py:90
  229.2 5.5 %fusion.59 = f32[8,256,1024]{1,2,0:T(8,128)} fusion(bf16[1,8,1,256,1024]{3,4,1,2,0:T(8,128)(2,1)S(1)} %fusion.5), kind=kOutput, calls=%fused_computation.79 | convolution fusion | flops 1074790400 | bytes 12582912 | tf_op jit(solution)/shard_map/zw,bwk->bzk/dot_general | solution.py:47
  234.7 5.5 %fusion.56 = f32[8,256,1024]{1,2,0:T(8,128)} fusion(bf16[1,8,1,256,1024]{3,4,1,2,0:T(8,128)(2,1)S(1)} %fusion.5), kind=kOutput, calls=%fused_computation.78 | convolution fusion | flops 1074790400 | bytes 12582912 | tf_op jit(solution)/shard_map/zw,bwk->bzk/dot_general | solution.py:46
  240.2 3.1 add_bitcast_fusion
  244.2 8.6 %fusion.21 = (bf16[8,256,512]{1,2,0:T(8,128)(2,1)}, bf16[8,256,512]{1,2,0:T(8,128)(2,1)}) fusion(f32[8,256,1024]{1,2,0:T(8,128)} %fusion.59, f32[8,256,1024]{1,2,0:T(8,128)} %fusion.56), kind=kLoop, calls=%fused_computation.45 | loop fusion | flops 4194304 | bytes 20971520 | tf_op jit(solution)/shard_map/convert
  252.8 50.2 %all-reduce.13.cloned.1.call-done = f32[1,256,512]{2,1,0:T(8,128)} async-done(((f32[1,256,512]{2,1,0:T(8,128)}), f32[1,256,512]{2,1,0:T(8,128)}) %all-reduce.13.cloned.1.call-update) | async-done | bytes 524304 | tf_op jit(solution)/shard_map/psum | solution.py:146
  303.0 1.2 maximum_divide_fusion
  304.3 3.4 fusion.76
  307.7 3.6 %collective-permute-start.3 = (f32[1,1,256,1024]{3,2,1,0:T(8,128)}, f32[1,1,256,1024]{3,2,1,0:T(8,128)S(1)}, u32[]{:S(2)}, u32[]{:S(2)}) collective-permute-start(f32[1,1,256,1024]{3,2,1,0:T(8,128)} %get-tuple-element.31), channel_id=1, source_target_pairs={{0,1},{1,2},{2,3},{3,4},{4,5},{5,6},{6,7},{7,8},{8,9},{9,10},{10,1... | collective-permute-start | bytes 3145736 | tf_op jit(solution)/shard_map/ppermute | solution.py:22
  311.4 4.7 %fusion.50 = f32[1,8,1,256,1024]{4,3,1,2,0:T(8,128)S(1)} fusion(bf16[8,256,512]{1,2,0:T(8,128)(2,1)S(1)} %copy-done.20, bf16[8,256,512]{1,2,0:T(8,128)(2,1)S(1)} %copy-done.19, bf16[512,512]{1,0:T(8,128)(2,1)S(1)} %copy-done.32, bf16[512,512]{1,0:T(8,128)(2,1)S(1)} %copy-done.24, bf16[512,512]{1,0:T(8,128)(2,1)S(1)} %copy-done.28), kind=kOutput, calls=%fused_computation.76 | convolution fusion | flops 4311744512 | bytes 14155776 | tf_op jit(solution)/shard_map/dot_general | solution.py:92
  316.1 1.9 fusion.18
  318.0 1.0 maximum_reduce_fusion.1
  319.0 15.8 %collective-permute-done.3 = f32[1,1,256,1024]{3,2,1,0:T(8,128)S(1)} collective-permute-done((f32[1,1,256,1024]{3,2,1,0:T(8,128)}, f32[1,1,256,1024]{3,2,1,0:T(8,128)S(1)}, u32[]{:S(2)}, u32[]{:S(2)}) %collective-permute-start.3) | collective-permute-done | bytes 1048608 | tf_op jit(solution)/shard_map/ppermute | solution.py:22
  334.8 3.1 fusion.78
  (85 shorter events, 4.1 us)
Async XLA Ops:
  6.5 10.6 %copy-start.3 = (f32[1,1,256,1024]{3,2,1,0:T(8,128)S(1)}, f32[1,1,256,1024]{3,2,1,0:T(8,128)}, u32[]{:S(2)}) copy-start(f32[1,1,256,1024]{3,2,1,0:T(8,128)} %param.7) | copy-start | bytes 3145732
  6.5 147.9 %all-reduce.11.cloned.1.call-start = ((), (), s32[]{:S(2)}) async-start(), calls=%async_computation | async-start | bytes 1048576 | tf_op jit(solution)/shard_map/psum | solution.py:146
  6.5 69.6 %collective-permute-start = (f32[1,1,256,1024]{3,2,1,0:T(8,128)}, f32[1,1,256,1024]{3,2,1,0:T(8,128)}, u32[]{:S(2)}, u32[]{:S(2)}) collective-permute-start(f32[1,1,256,1024]{3,2,1,0:T(8,128)} %param.7), channel_id=1, source_target_pairs={{1,0},{2,1},{3,2},{4,3},{5,4},{6,5},{7,6},{8,7},{9,8},{10,9},{11,1... | collective-permute-start | bytes 3145736 | tf_op jit(solution)/shard_map/ppermute | solution.py:22
  15.2 9.4 %copy-start.21 = (bf16[512,512]{1,0:T(8,128)(2,1)}, bf16[512,512]{1,0:T(8,128)(2,1)S(1)}, u32[]{:S(2)}) copy-start(bf16[512,512]{1,0:T(8,128)(2,1)S(1)} %fusion.94) | copy-start | bytes 1572868
  15.2 7.9 %copy-start = (bf16[8,1,256,1024]{3,2,1,0:T(8,128)(2,1)S(1)}, bf16[8,1,256,1024]{3,2,1,0:T(8,128)(2,1)}, u32[]{:S(2)}) copy-start(bf16[8,1,256,1024]{3,2,1,0:T(8,128)(2,1)} %param.5) | copy-start | bytes 12582916
  23.0 1.6 copy-start.25
  23.0 1.6 copy-start.29
  34.7 5.5 %copy-start.33 = (s32[1,256,18]{1,0,2:T(1,128)S(1)}, s32[1,256,18]{1,0,2:T(1,128)}, u32[]{:S(2)}) copy-start(s32[1,256,18]{1,0,2:T(1,128)} %param.6) | copy-start | bytes 55300
  50.0 10.5 %copy-start.4 = (bf16[1,8,1,256,1024]{3,4,1,2,0:T(8,128)(2,1)S(1)}, bf16[1,8,1,256,1024]{3,4,1,2,0:T(8,128)(2,1)}, u32[]{:S(2)}) copy-start(bf16[1,8,1,256,1024]{3,4,1,2,0:T(8,128)(2,1)} %copy.14) | copy-start | bytes 12582916
  70.7 5.5 %copy-start.10 = (f32[1,1,256,1023]{3,2,1,0:T(8,128)S(1)}, f32[1,1,256,1023]{3,2,1,0:T(8,128)}, u32[]{:S(2)}) copy-start(f32[1,1,256,1023]{3,2,1,0:T(8,128)} %slice_subtract_fusion.6) | copy-start | bytes 3142660
  79.4 223.6 %all-reduce.13.cloned.1.call-start = ((), (), s32[]{:S(2)}) async-start(), calls=%async_computation.1 | async-start | bytes 1048576 | tf_op jit(solution)/shard_map/psum | solution.py:146
  155.7 5.2 %copy-start.17 = (bf16[8,256,512]{1,2,0:T(8,128)(2,1)S(1)}, bf16[8,256,512]{1,2,0:T(8,128)(2,1)}, u32[]{:S(2)}) copy-start(bf16[8,256,512]{1,2,0:T(8,128)(2,1)} %get-tuple-element.13) | copy-start | bytes 6291460
  155.7 5.2 %copy-start.18 = (bf16[8,256,512]{1,2,0:T(8,128)(2,1)S(1)}, bf16[8,256,512]{1,2,0:T(8,128)(2,1)}, u32[]{:S(2)}) copy-start(bf16[8,256,512]{1,2,0:T(8,128)(2,1)} %get-tuple-element.14) | copy-start | bytes 6291460
  155.7 5.2 %copy-start.22 = (bf16[512,512]{1,0:T(8,128)(2,1)S(1)}, bf16[512,512]{1,0:T(8,128)(2,1)}, u32[]{:S(2)}) copy-start(bf16[512,512]{1,0:T(8,128)(2,1)} %copy-done.21) | copy-start | bytes 1572868
  155.7 5.2 %copy-start.26 = (bf16[512,512]{1,0:T(8,128)(2,1)S(1)}, bf16[512,512]{1,0:T(8,128)(2,1)}, u32[]{:S(2)}) copy-start(bf16[512,512]{1,0:T(8,128)(2,1)} %copy-done.25) | copy-start | bytes 1572868
  155.7 5.2 %copy-start.30 = (bf16[512,512]{1,0:T(8,128)(2,1)S(1)}, bf16[512,512]{1,0:T(8,128)(2,1)}, u32[]{:S(2)}) copy-start(bf16[512,512]{1,0:T(8,128)(2,1)} %copy-done.29) | copy-start | bytes 1572868
  158.1 29.0 %copy-start.6 = (f32[1,1,256,1024]{3,2,1,0:T(8,128)}, f32[1,1,256,1024]{3,2,1,0:T(8,128)S(1)}, u32[]{:S(2)}) copy-start(f32[1,1,256,1024]{3,2,1,0:T(8,128)S(1)} %get-tuple-element.35) | copy-start | bytes 3145732
  158.1 29.0 %copy-start.8 = (f32[1,1,256,1024]{3,2,1,0:T(8,128)}, f32[1,1,256,1024]{3,2,1,0:T(8,128)S(1)}, u32[]{:S(2)}) copy-start(f32[1,1,256,1024]{3,2,1,0:T(8,128)S(1)} %get-tuple-element.36) | copy-start | bytes 3145732
  158.1 29.0 %copy-start.13 = (f32[1,1,256,1024]{3,2,1,0:T(8,128)}, f32[1,1,256,1024]{3,2,1,0:T(8,128)S(1)}, u32[]{:S(2)}) copy-start(f32[1,1,256,1024]{3,2,1,0:T(8,128)S(1)} %get-tuple-element.34) | copy-start | bytes 3145732
  158.1 28.9 %collective-permute-start.1 = (f32[1,1,256,1024]{3,2,1,0:T(8,128)S(1)}, f32[1,1,256,1024]{3,2,1,0:T(8,128)S(1)}, u32[]{:S(2)}, u32[]{:S(2)}) collective-permute-start(f32[1,1,256,1024]{3,2,1,0:T(8,128)S(1)} %get-tuple-element.34), channel_id=1, source_target_pairs={{0,1},{1,2},{2,3},{3,4},{4,5},{5,6},{6,7},{7,8},{8,9},{9,10},{10,1... | collective-permute-start | bytes 3145736 | tf_op jit(solution)/shard_map/ppermute | solution.py:22
  160.9 4.7 %copy-start.1 = (bf16[8,1,256,1024]{3,2,1,0:T(8,128)(2,1)S(1)}, bf16[8,1,256,1024]{3,2,1,0:T(8,128)(2,1)}, u32[]{:S(2)}) copy-start(bf16[8,1,256,1024]{3,2,1,0:T(8,128)(2,1)} %param.5) | copy-start | bytes 12582916
  191.4 48.8 %collective-permute-start.2 = (f32[1,1,256,1024]{3,2,1,0:T(8,128)S(1)}, f32[1,1,256,1024]{3,2,1,0:T(8,128)}, u32[]{:S(2)}, u32[]{:S(2)}) collective-permute-start(f32[1,1,256,1024]{3,2,1,0:T(8,128)S(1)} %get-tuple-element.7), channel_id=1, source_target_pairs={{1,0},{2,1},{3,2},{4,3},{5,4},{6,5},{7,6},{8,7},{9,8},{10,9},{11,1... | collective-permute-start | bytes 3145736 | tf_op jit(solution)/shard_map/ppermute | solution.py:22
  194.0 1.5 copy-start.23
  194.1 1.5 copy-start.27
  194.1 1.5 copy-start.31
  211.1 10.6 %copy-start.5 = (bf16[1,8,1,256,1024]{3,4,1,2,0:T(8,128)(2,1)S(1)}, bf16[1,8,1,256,1024]{3,4,1,2,0:T(8,128)(2,1)}, u32[]{:S(2)}) copy-start(bf16[1,8,1,256,1024]{3,4,1,2,0:T(8,128)(2,1)} %copy.14) | copy-start | bytes 12582916
  211.1 10.6 %copy-start.15 = (f32[256,1024]{0,1:T(8,128)S(1)}, f32[256,1024]{0,1:T(8,128)}, u32[]{:S(2)}) copy-start(f32[256,1024]{0,1:T(8,128)} %fusion.70) | copy-start | bytes 3145732
  234.7 5.5 %copy-start.7 = (f32[1,1,256,1024]{3,2,1,0:T(8,128)S(1)}, f32[1,1,256,1024]{3,2,1,0:T(8,128)}, u32[]{:S(2)}) copy-start(f32[1,1,256,1024]{3,2,1,0:T(8,128)} %copy-done.6) | copy-start | bytes 3145732
  234.7 5.5 %copy-start.9 = (f32[1,1,256,1024]{3,2,1,0:T(8,128)S(1)}, f32[1,1,256,1024]{3,2,1,0:T(8,128)}, u32[]{:S(2)}) copy-start(f32[1,1,256,1024]{3,2,1,0:T(8,128)} %copy-done.8) | copy-start | bytes 3145732
  234.7 5.5 %copy-start.11 = (f32[1,1,255,1024]{3,2,1,0:T(8,128)S(1)}, f32[1,1,255,1024]{3,2,1,0:T(8,128)}, u32[]{:S(2)}) copy-start(f32[1,1,255,1024]{3,2,1,0:T(8,128)} %slice_subtract_fusion.5) | copy-start | bytes 3133444
  234.7 5.5 %copy-start.12 = (f32[1,1,256,1023]{3,2,1,0:T(8,128)S(1)}, f32[1,1,256,1023]{3,2,1,0:T(8,128)}, u32[]{:S(2)}) copy-start(f32[1,1,256,1023]{3,2,1,0:T(8,128)} %slice_subtract_fusion.4) | copy-start | bytes 3142660
  234.7 5.5 %copy-start.14 = (f32[1,1,256,1024]{3,2,1,0:T(8,128)S(1)}, f32[1,1,256,1024]{3,2,1,0:T(8,128)}, u32[]{:S(2)}) copy-start(f32[1,1,256,1024]{3,2,1,0:T(8,128)} %copy-done.13) | copy-start | bytes 3145732
  304.2 7.1 %copy-start.19 = (bf16[8,256,512]{1,2,0:T(8,128)(2,1)S(1)}, bf16[8,256,512]{1,2,0:T(8,128)(2,1)}, u32[]{:S(2)}) copy-start(bf16[8,256,512]{1,2,0:T(8,128)(2,1)} %get-tuple-element.9) | copy-start | bytes 6291460
  304.2 7.1 %copy-start.20 = (bf16[8,256,512]{1,2,0:T(8,128)(2,1)S(1)}, bf16[8,256,512]{1,2,0:T(8,128)(2,1)}, u32[]{:S(2)}) copy-start(bf16[8,256,512]{1,2,0:T(8,128)(2,1)} %get-tuple-element.10) | copy-start | bytes 6291460
  304.2 7.1 %copy-start.24 = (bf16[512,512]{1,0:T(8,128)(2,1)S(1)}, bf16[512,512]{1,0:T(8,128)(2,1)}, u32[]{:S(2)}) copy-start(bf16[512,512]{1,0:T(8,128)(2,1)} %copy-done.21) | copy-start | bytes 1572868
  304.3 7.1 %copy-start.28 = (bf16[512,512]{1,0:T(8,128)(2,1)S(1)}, bf16[512,512]{1,0:T(8,128)(2,1)}, u32[]{:S(2)}) copy-start(bf16[512,512]{1,0:T(8,128)(2,1)} %copy-done.25) | copy-start | bytes 1572868
  304.3 7.1 %copy-start.32 = (bf16[512,512]{1,0:T(8,128)(2,1)S(1)}, bf16[512,512]{1,0:T(8,128)(2,1)}, u32[]{:S(2)}) copy-start(bf16[512,512]{1,0:T(8,128)(2,1)} %copy-done.29) | copy-start | bytes 1572868
  307.7 27.1 %collective-permute-start.3 = (f32[1,1,256,1024]{3,2,1,0:T(8,128)}, f32[1,1,256,1024]{3,2,1,0:T(8,128)S(1)}, u32[]{:S(2)}, u32[]{:S(2)}) collective-permute-start(f32[1,1,256,1024]{3,2,1,0:T(8,128)} %get-tuple-element.31), channel_id=1, source_target_pairs={{0,1},{1,2},{2,3},{3,4},{4,5},{5,6},{6,7},{7,8},{8,9},{9,10},{10,1... | collective-permute-start | bytes 3145736 | tf_op jit(solution)/shard_map/ppermute | solution.py:22
  311.4 4.7 %copy-start.2 = (bf16[8,1,256,1024]{3,2,1,0:T(8,128)(2,1)S(1)}, bf16[8,1,256,1024]{3,2,1,0:T(8,128)(2,1)}, u32[]{:S(2)}) copy-start(bf16[8,1,256,1024]{3,2,1,0:T(8,128)(2,1)} %param.5) | copy-start | bytes 12582916
  318.0 16.8 %copy-start.16 = (f32[1,1,256,1024]{3,2,1,0:T(8,128)S(1)}, f32[1,1,256,1024]{3,2,1,0:T(8,128)}, u32[]{:S(2)}) copy-start(f32[1,1,256,1024]{3,2,1,0:T(8,128)} %get-tuple-element.8) | copy-start | bytes 3145732
Sparse Core Ops, SparseCore 0:
  79.6 61.5 all-reduce.10
  244.3 58.6 all-reduce.12
where the time goes:
time: 349 us; the launch traced here: 345 us
  other arithmetic  96.1 us (28%)
  waiting for transfers between devices  84.8 us (24%)
  blocking collectives  65.6 us (19%)
  matrix products  62.3 us (18%)
  between operations  14.9 us (4%)
  starting transfers between devices  13.6 us (4%)
  local copies, waits for them, and re-layouts  7.7 us (2%)
    psum x1, blocking collectives, shards(): power = lax.psum(power_local, ('echo', 'plane'))  65.6 us
    psum x2, waiting for transfers between devices, shards(): total = lax.psum(squares, 'echo')  50.2 us
    ppermute x4, waiting for transfers between devices, passed_along(): return lax.ppermute(value, axis, pairs)  34.5 us
    dot_general x4, matrix products, along_kz(): jnp.einsum('zw,bwk->bzk', sine, half, preferred_element_type=jnp.float32)  22 us
    dot_general x4, matrix products, along_kz(): jnp.einsum('zw,bwk->bzk', cosine, half, preferred_element_type=jnp.float32)  21.9 us
    add x2, other arithmetic, along_kz(): real_part = first[..., :width] + second[..., width:]  21.1 us
    another operation x4, other arithmetic  20.1 us
    ppermute x4, starting transfers between devices, passed_along(): return lax.ppermute(value, axis, pairs)  13.6 us
  transfers between devices with their start and end apart: 6, of which 3 were waited for; matrix products, arithmetic and copies ran while one was open for 41% of the time, Pallas kernels for 0%

commit v1 on v0

v1 whole, which is shorter than its diff:
```python
import functools
import math

import jax
import jax.numpy as jnp
import ml_dtypes
import numpy as np
from jax import lax
from jax.experimental import pallas as pl
from jax.experimental.pallas import tpu as pltpu
from jax.sharding import PartitionSpec as P

NY = 512
NZ = 256
COILS = 8
RADIUS_FACTOR = 0.5
EPSILON = 1e-06
ROWS = 16
CHUNKS = NZ // ROWS
JOBS = 2 * CHUNKS
MESH = pl.DeviceIdType.MESH
bf16 = jnp.bfloat16
f32 = jnp.float32

LAG_SEND = 3
START_PRIMAL = 16
START_SECOND = 28
START_COILS = 32
START_FINAL = 48
STEPS = START_FINAL + CHUNKS


def tables(count):
    index = np.arange(count, dtype=np.int64)
    angle = ((index[:, None] * index[None, :]) % count).astype(np.float32) * np.float32(
        2.0 * math.pi / count
    )
    scale = np.float32(1.0 / math.sqrt(count))
    return tuple(
        (part(angle).astype(np.float32) * scale).astype(ml_dtypes.bfloat16)
        for part in (np.cos, np.sin)
    )


def constants():
    cos_y, sin_y = tables(NY)
    cos_z, sin_z = tables(NZ)
    ky_forward, ky_inverse, kz_forward, kz_inverse = [], [], [], []
    for q in range(4):
        c, s = cos_y[:128, q::4], sin_y[:128, q::4]
        ky_forward.append(np.block([[c, -s], [s, c]]))
        ky_inverse.append(np.block([[c.T, s.T], [-s.T, c.T]]))
    for p in range(2):
        c, s = cos_z[p::2, :128], sin_z[p::2, :128]
        kz_forward.append(np.block([[c, s], [-s, c]]))
        kz_inverse.append(kz_forward[-1].T)
    rows = np.zeros((NZ, NZ), np.float32)
    for r in range(NZ):
        rows[r, (r % 128) * 2 + r // 128] = 1
    lanes = np.zeros((NY, NY), np.float32)
    for k in range(NY):
        lanes[k, (k % 4) * 128 + k // 4] = 1
    lane = np.arange(NY)
    ky = 4 * (lane % 128) + lane // 128
    where = np.zeros((8, NY), np.int32)
    where[0] = ky // 30
    where[1] = ky % 30
    cast = lambda a: np.ascontiguousarray(np.stack(a)).astype(ml_dtypes.bfloat16)
    return (
        cast(ky_forward),
        cast(ky_inverse),
        cast(kz_forward),
        cast(kz_inverse),
        rows.astype(ml_dtypes.bfloat16),
        lanes.astype(ml_dtypes.bfloat16),
        where,
    )


def dot(a, b):
    return jnp.dot(a, b, preferred_element_type=f32)


def permute_acquired(c, acq, acqp, rows, lanes, tmp):
    for n in range(4):
        sl = slice(n * 256, (n + 1) * 256)
        tmp[:, sl] = dot(rows[...], acq[c, :, sl]).astype(bf16)
    for part in range(2):
        for n in range(2):
            v = dot(
                tmp[:, part * 512 : (part + 1) * 512], lanes[:, n * 256 : (n + 1) * 256]
            ).astype(bf16)
            out = (slice(part * 128, (part + 1) * 128), slice(n * 256, (n + 1) * 256))
            acqp[(c, 0) + out] = v[:128]
            acqp[(c, 1) + out] = v[128:]


def coil_image(c, w, maps, xs):
    def body(b, _):
        r = pl.ds(pl.multiple_of(b * 16, 16), 16)
        xr, xi = [], []
        for t in range(4):
            l = slice(t * 128, (t + 1) * 128)
            h = slice(512 + t * 128, 512 + (t + 1) * 128)
            mr, mi = maps[c, r, l].astype(f32), maps[c, r, h].astype(f32)
            wr, wi = w[r, l], w[r, h]
            xr.append(mr * wr - mi * wi)
            xi.append(mr * wi + mi * wr)
        ar, ai, br, bi = xr[0] + xr[2], xi[0] + xi[2], xr[0] - xr[2], xi[0] - xi[2]
        cr, ci, dr, di = xr[1] + xr[3], xi[1] + xi[3], xr[1] - xr[3], xi[1] - xi[3]
        outs = [(ar + cr, ai + ci), (br + di, bi - dr), (ar - cr, ai - ci), (br - di, bi + dr)]
        for q, (re, im) in enumerate(outs):
            xs[r, q * 256 : q * 256 + 128] = re.astype(bf16)
            xs[r, q * 256 + 128 : q * 256 + 256] = im.astype(bf16)
        return 0

    lax.fori_loop(0, NZ // 16, body, 0, unroll=2)


def ky_forward(xs, kf, hs):
    for q in range(4):
        h = dot(xs[:, q * 256 : (q + 1) * 256], kf[q])
        s = (h[:128] + h[128:]).astype(bf16)
        d = (h[:128] - h[128:]).astype(bf16)
        l = slice(q * 128, (q + 1) * 128)
        hs[0, 0:128, l] = s[:, :128]
        hs[0, 128:256, l] = s[:, 128:]
        hs[1, 0:128, l] = d[:, :128]
        hs[1, 128:256, l] = d[:, 128:]


def kz_residual(c, hs, tf, acqp, mask, rs):
    for p in range(2):
        for n in range(2):
            l = slice(n * 256, (n + 1) * 256)
            y = dot(tf[p], hs[p, :, l])
            m = mask[p, :, l]
            for i in range(2):
                rr = slice(i * 128, (i + 1) * 128)
                rs[p, rr, l] = (y[rr] - acqp[c, p, rr, l].astype(f32)).astype(bf16) * m


def kz_inverse(rs, ti, hp):
    for n in range(2):
        l = slice(n * 256, (n + 1) * 256)
        e, o = dot(ti[0], rs[0, :, l]), dot(ti[1], rs[1, :, l])
        for first, v in ((0, (e + o).astype(bf16)), (128, (e - o).astype(bf16))):
            for k in range(2):
                base = (2 * n + k) * 256
                ll = slice(k * 128, (k + 1) * 128)
                hp[first : first + 128, base : base + 128] = v[:128, ll]
                hp[first : first + 128, base + 128 : base + 256] = v[128:, ll]


def ky_inverse(hp, ki, zs):
    for q in range(4):
        zs[:, q * 256 : (q + 1) * 256] = dot(hp[:, q * 256 : (q + 1) * 256], ki[q])


def coil_sum(c, zs, maps, d):
    def body(b, _):
        r = pl.ds(pl.multiple_of(b * 16, 16), 16)
        g = [(zs[r, q * 256 : q * 256 + 128], zs[r, q * 256 + 128 : q * 256 + 256]) for q in range(4)]
        ar, ai, br, bi = g[0][0] + g[2][0], g[0][1] + g[2][1], g[0][0] - g[2][0], g[0][1] - g[2][1]
        cr, ci, dr, di = g[1][0] + g[3][0], g[1][1] + g[3][1], g[1][0] - g[3][0], g[1][1] - g[3][1]
        z = [(ar + cr, ai + ci), (br - di, bi + dr), (ar - cr, ai - ci), (br + di, bi - dr)]
        for t in range(4):
            l = slice(t * 128, (t + 1) * 128)
            h = slice(512 + t * 128, 512 + (t + 1) * 128)
            mr, mi = maps[c, r, l].astype(f32), maps[c, r, h].astype(f32)
            zr, zi = z[t]
            d[r, l] += mr * zr + mi * zi
            d[r, h] += mr * zi - mi * zr
        return 0

    lax.fori_loop(0, NZ // 16, body, 0, unroll=2)


def build_mask(words, where, mask):
    column = where[0:1, :]
    bit = where[1:2, :]
    for p in range(2):
        for b in range(8):
            part = words[pl.ds(p + 32 * b, 16, stride=2), :]
            spread = jnp.zeros((16, NY), jnp.int32)
            for w in range(18):
                spread = jnp.where(column == w, part[:, w : w + 1], spread)
            value = jnp.right_shift(spread, jnp.broadcast_to(bit, (16, NY))) & 1
            mask[p, 16 * b : 16 * b + 16, :] = value.astype(f32).astype(bf16)


def kernel(
    acq_hbm, maps_hbm, words_hbm, u_hbm, kf_hbm, ki_hbm, tf_hbm, ti_hbm, rows_hbm, lanes_hbm, where_hbm,
    out_hbm,
    acq, maps, words, kf, ki, tf, ti, rows, lanes, where,
    acqp, mask, xs, hs, rs, hp, zs,
    cur, extra, w, d, px, pz, py, upb, pxprev,
    n2, crecv, half, xrecv, tot, pw, pw_recv, rad,
    in_sem, up_s, up_r, px_s, px_r, cs, cr, xsend, xrecv_sem, as_, ar, ps, pr, out_sem,
):
    e = lax.axis_index("echo")
    p = lax.axis_index("plane")
    core, x = lax.rem(e, 2), e // 2
    y, z = lax.rem(p, 4), p // 4
    has_up, has_down = p < 15, p > 0
    partner = (e + 1 - 2 * core, p)
    others_x = [(lax.rem(x + k, 4) * 2 + core, p) for k in (1, 2, 3)]
    others_y = [(e, z * 4 + lax.rem(y + k, 4)) for k in (1, 2, 3)]
    others_z = [(e, lax.rem(z + k, 4) * 4 + y) for k in (1, 2, 3)]
    up, down = (e, p + 1), (e, p - 1)

    barrier = pltpu.get_barrier_semaphore()
    greet = [partner] + others_x + others_y + others_z
    for device in greet:
        pl.semaphore_signal(barrier, inc=1, device_id=device, device_id_type=MESH)

    @pl.when(has_up)
    def _():
        pl.semaphore_signal(barrier, inc=1, device_id=up, device_id_type=MESH)

    @pl.when(has_down)
    def _():
        pl.semaphore_signal(barrier, inc=1, device_id=down, device_id_type=MESH)

    loads = [(u_hbm, cur), (words_hbm, words), (where_hbm, where), (rows_hbm, rows), (lanes_hbm, lanes)]
    loads += [(kf_hbm, kf), (tf_hbm, tf), (ti_hbm, ti), (ki_hbm, ki)]
    for c in range(COILS):
        loads += [(acq_hbm.at[c], acq.at[c]), (maps_hbm.at[c], maps.at[c])]
    copies = [pltpu.make_async_copy(a, b, in_sem.at[i]) for i, (a, b) in enumerate(loads)]
    for copy in copies:
        copy.start()

    px[...] = jnp.zeros_like(px)
    pz[...] = jnp.zeros_like(pz)
    py[...] = jnp.zeros_like(py)
    d[...] = jnp.zeros_like(d)
    extra[NZ : NZ + 8, :] = jnp.zeros((8, 2 * NY), f32)

    pl.semaphore_wait(barrier, len(greet) + has_up.astype(jnp.int32) + has_down.astype(jnp.int32))

    def span(c, offset=0):
        return pl.ds(pl.multiple_of(c * ROWS + offset, 8), ROWS)

    def send_up(j, source):
        it, c = j // CHUNKS, lax.rem(j, CHUNKS)
        return pltpu.make_async_remote_copy(
            src_ref=source.at[span(c)],
            dst_ref=upb.at[it, span(c)],
            send_sem=up_s.at[j],
            recv_sem=up_r.at[j],
            device_id=down,
            device_id_type=MESH,
        )

    def send_dual(j):
        it, c = j // CHUNKS, lax.rem(j, CHUNKS)
        return pltpu.make_async_remote_copy(
            src_ref=px.at[span(c)],
            dst_ref=pxprev.at[it, span(c)],
            send_sem=px_s.at[j],
            recv_sem=px_r.at[j],
            device_id=up,
            device_id_type=MESH,
        )

    mine = pl.ds(pl.multiple_of(core * 8, 8), 8)
    theirs = pl.ds(pl.multiple_of(8 - core * 8, 8), 8)

    def send_half(j):
        return pltpu.make_async_remote_copy(
            src_ref=n2.at[j, theirs],
            dst_ref=crecv.at[j],
            send_sem=cs.at[j],
            recv_sem=cr.at[j],
            device_id=partner,
            device_id_type=MESH,
        )

    def send_x(j, k):
        return pltpu.make_async_remote_copy(
            src_ref=half.at[j],
            dst_ref=xrecv.at[k, j],
            send_sem=xsend.at[k, j],
            recv_sem=xrecv_sem.at[k, j],
            device_id=others_x[k],
            device_id_type=MESH,
        )

    def send_total(j):
        return pltpu.make_async_remote_copy(
            src_ref=tot.at[j, mine],
            dst_ref=tot.at[j, mine],
            send_sem=as_.at[j],
            recv_sem=ar.at[j],
            device_id=partner,
            device_id_type=MESH,
        )

    power_groups = [[partner], others_x, others_y, others_z]
    power_first = [0, 1, 4, 7]

    def send_power(stage, k):
        slot = power_first[stage] + k
        return pltpu.make_async_remote_copy(
            src_ref=pw.at[stage],
            dst_ref=pw_recv.at[slot],
            send_sem=ps.at[slot],
            recv_sem=pr.at[slot],
            device_id=power_groups[stage][k],
            device_id_type=MESH,
        )

    @pl.when(has_down)
    def _():
        def body(j, _):
            send_up(j, u_hbm).start()
            return 0

        lax.fori_loop(0, CHUNKS, body, 0)

    copies[0].wait()

    def power_body(b, total):
        r = pl.ds(pl.multiple_of(b * 8, 8), 8)
        v = cur[r, :]
        extra[r, :] = v
        w[r, :] = v
        s = v * v
        for k in range(8):
            total = total + s[:, k * 128 : (k + 1) * 128]
        return total

    pw[0] = lax.fori_loop(0, NZ // 8, power_body, jnp.zeros((8, 128), f32), unroll=2)
    send_power(0, 0).start()
    for copy in copies[1:9]:
        copy.wait()
    build_mask(words, where, mask)

    lane = lax.broadcasted_iota(jnp.int32, (ROWS, 2 * NY), 1) & (NY - 1)
    row = lax.broadcasted_iota(jnp.int32, (ROWS, 2 * NY), 0)

    def squares(j):
        it, c = j // CHUNKS, lax.rem(j, CHUNKS)

        @pl.when(has_up)
        def _():
            send_up(j, extra).wait_recv()

            @pl.when(it == 1)
            def _():
                send_dual(j - CHUNKS).wait_send()

        r = span(c)
        wide = extra[pl.ds(pl.multiple_of(c * ROWS, 8), ROWS + 8), :]
        here = wide[:ROWS]
        gx = jnp.where(has_up, upb[it, r, :] - here, 0.0)
        gz = jnp.where(row + c * ROWS < NZ - 1, wide[1 : ROWS + 1] - here, 0.0)
        gy = jnp.where(lane < NY - 1, pltpu.roll(here, 2 * NY - 1, 1) - here, 0.0)
        rz = span(c, 8)
        vx = px[r, :] + 0.25 * gx
        vz = pz[rz, :] + 0.25 * gz
        vy = py[r, :] + 0.25 * gy
        px[r, :] = vx
        pz[rz, :] = vz
        py[r, :] = vy
        s = vx * vx + vz * vz + vy * vy
        n2[j] = s[:, :NY] + s[:, NY:]
        send_half(j).start()

    def halves(j):
        send_half(j).wait_recv()
        half[j] = n2[j, mine, :] + crecv[j]
        for k in range(3):
            send_x(j, k).start()

    def totals(j):
        for k in range(3):
            send_x(j, k).wait_recv()
        tot[j, mine, :] = (half[j] + xrecv[0, j]) + (xrecv[1, j] + xrecv[2, j])
        send_total(j).start()

    def shrink(j):
        c = lax.rem(j, CHUNKS)
        send_total(j).wait_recv()
        s = jnp.minimum(1.0, rad[0:1, 0:1] * lax.rsqrt(tot[j]))
        s = jnp.concatenate([s, s], 1)
        r, rz = span(c), span(c, 8)
        px[r, :] = px[r, :] * s
        pz[rz, :] = pz[rz, :] * s
        py[r, :] = py[r, :] * s

        @pl.when(has_up)
        def _():
            send_dual(j).start()

    def primal(j):
        it, c = j // CHUNKS, lax.rem(j, CHUNKS)

        @pl.when(has_down)
        def _():
            send_dual(j).wait_recv()

        r = span(c)
        below = jnp.where(has_down, pxprev[it, r, :], 0.0)
        wide = pz[pl.ds(pl.multiple_of(c * ROWS, 8), ROWS + 8), :]
        vy = py[r, :]
        before = jnp.where(lane > 0, pltpu.roll(vy, 1, 1), 0.0)
        g = (below - px[r, :]) + (wide[7 : ROWS + 7] - wide[8:]) + (before - vy)
        factor = jnp.where(it == 0, 0.2, 0.36).astype(f32)
        old = cur[r, :]
        new = old - 0.25 * (factor * d[r, :] + g)
        cur[r, :] = new

        @pl.when(it == 0)
        def _():
            ahead = 2.0 * new - old
            extra[r, :] = ahead
            w[r, :] = (0.2 / 0.36) * ahead + (0.16 / 0.36) * old
            d[r, :] = jnp.zeros((ROWS, 2 * NY), f32)

            @pl.when(has_down)
            def _():
                send_up(j + CHUNKS, extra).start()

        @pl.when(it == 1)
        def _():
            store(c).start()

    def store(c):
        return pltpu.make_async_copy(cur.at[span(c)], out_hbm.at[span(c)], out_sem.at[c])

    def coil_first(it, c):
        @pl.when(it == 0)
        def _():
            pltpu.make_async_copy(acq_hbm.at[c], acq.at[c], in_sem.at[9 + 2 * c]).wait()
            pltpu.make_async_copy(maps_hbm.at[c], maps.at[c], in_sem.at[10 + 2 * c]).wait()
            permute_acquired(c, acq, acqp, rows, lanes, xs)

        coil_image(c, w, maps, xs)
        ky_forward(xs, kf, hs)

    def coil_second(c):
        kz_residual(c, hs, tf, acqp, mask, rs)
        kz_inverse(rs, ti, hp)
        ky_inverse(hp, ki, zs)
        coil_sum(c, zs, maps, d)

    def step(t, _):
        for stage in range(4):

            @pl.when(t == stage)
            def _(stage=stage):
                total = pw[stage]
                for k in range(len(power_groups[stage])):
                    send_power(stage, k).wait_recv()
                    total = total + pw_recv[power_first[stage] + k]
                if stage < 3:
                    pw[stage + 1] = total
                    for k in range(3):
                        send_power(stage + 1, k).start()
                else:
                    mean = jnp.sum(total) * (1.0 / 16777216.0) + EPSILON
                    rad[...] = RADIUS_FACTOR * jnp.sqrt(jnp.broadcast_to(mean, (8, 128)))

        first = t - START_SECOND + CHUNKS

        def job(lag):
            a, b = t - lag, first - lag
            valid_a = (a >= 0) & (a < CHUNKS)
            valid_b = (b >= CHUNKS) & (b < JOBS)
            return valid_a | valid_b, jnp.where(valid_a, a, b)

        def run(lag, work):
            valid, j = job(lag)

            @pl.when(valid)
            def _():
                work(j)

        run(2, totals)
        run(0, squares)
        second = t >= START_COILS
        it = second.astype(jnp.int32)
        part = t - jnp.where(second, START_COILS, 0)

        @pl.when((part < 2 * COILS) & (lax.rem(part, 2) == 0))
        def _():
            coil_first(it, part // 2)

        @pl.when((part < 2 * COILS) & (lax.rem(part, 2) == 1))
        def _():
            coil_second(part // 2)

        run(0, halves)
        run(LAG_SEND, shrink)

        a, b = t - START_PRIMAL, t - START_FINAL
        valid_a = (a >= 0) & (a < CHUNKS)

        @pl.when(valid_a | (b >= 0))
        def _():
            primal(jnp.where(valid_a, a, b + CHUNKS))

        return 0

    lax.fori_loop(0, STEPS, step, 0)

    for stage in range(4):
        for k in range(len(power_groups[stage])):
            send_power(stage, k).wait_send()

    def drain(j, _):
        send_half(j).wait_send()
        for k in range(3):
            send_x(j, k).wait_send()
        send_total(j).wait_send()

        @pl.when(has_down)
        def _():
            send_up(j, extra).wait_send()

        @pl.when(has_up & (j >= CHUNKS))
        def _():
            send_dual(j).wait_send()

        @pl.when(j < CHUNKS)
        def _():
            store(j).wait()

        return 0

    lax.fori_loop(0, JOBS, drain, 0)


def shards(acquired, coil_maps, mask_words, start_image):
    acquired = acquired.reshape(COILS, NZ, 2 * NY)
    coil_maps = coil_maps.reshape(COILS, NZ, 2 * NY)
    words = mask_words.reshape(NZ, 18)
    image = start_image.reshape(NZ, 2 * NY)
    consts = [jnp.asarray(a) for a in constants()]
    anywhere = pl.BlockSpec(memory_space=pl.ANY)
    vmem = lambda shape, dtype=f32: pltpu.VMEM(shape, dtype)
    dma = lambda *shape: pltpu.SemaphoreType.DMA(shape)
    scratch = [
        vmem((COILS, NZ, 2 * NY), bf16),
        vmem((COILS, NZ, 2 * NY), bf16),
        vmem((NZ, 18), jnp.int32),
        vmem((4, 256, 256), bf16),
        vmem((4, 256, 256), bf16),
        vmem((2, 256, 256), bf16),
        vmem((2, 256, 256), bf16),
        vmem((256, 256), bf16),
        vmem((512, 512), bf16),
        vmem((8, NY), jnp.int32),
        vmem((COILS, 2, 256, 512), bf16),
        vmem((2, 128, 512), bf16),
        vmem((256, 1024), bf16),
        vmem((2, 256, 512), bf16),
        vmem((2, 256, 512), bf16),
        vmem((256, 1024), bf16),
        vmem((256, 1024)),
        vmem((NZ, 2 * NY)),
        vmem((NZ + 8, 2 * NY)),
        vmem((NZ, 2 * NY)),
        vmem((NZ, 2 * NY)),
        vmem((NZ, 2 * NY)),
        vmem((NZ + 8, 2 * NY)),
        vmem((NZ, 2 * NY)),
        vmem((2, NZ, 2 * NY)),
        vmem((2, NZ, 2 * NY)),
        vmem((JOBS, ROWS, NY)),
        vmem((JOBS, 8, NY)),
        vmem((JOBS, 8, NY)),
        vmem((3, JOBS, 8, NY)),
        vmem((JOBS, ROWS, NY)),
        vmem((4, 8, 128)),
        vmem((10, 8, 128)),
        vmem((8, 128)),
        dma(9 + 2 * COILS),
        dma(JOBS),
        dma(JOBS),
        dma(JOBS),
        dma(JOBS),
        dma(JOBS),
        dma(JOBS),
        dma(3, JOBS),
        dma(3, JOBS),
        dma(JOBS),
        dma(JOBS),
        dma(10),
        dma(10),
        dma(CHUNKS),
    ]
    solved = pl.pallas_call(
        kernel,
        out_shape=jax.ShapeDtypeStruct((NZ, 2 * NY), f32),
        in_specs=[anywhere] * 11,
        out_specs=anywhere,
        scratch_shapes=scratch,
        compiler_params=pltpu.CompilerParams(
            collective_id=0, has_side_effects=True, vmem_limit_bytes=60 * 2**20
        ),
        name="solve",
    )(acquired, coil_maps, words, image, *consts)
    return solved.reshape(start_image.shape)


def solution(mesh):
    in_specs = (
        P("echo", None, "plane", None, None),
        P(None, "plane", None, None),
        P("echo", None, None),
        P("echo", "plane", None, None),
    )
    out_specs = P("echo", "plane", None, None)
    return jax.shard_map(shards, mesh=mesh, in_specs=in_specs, out_specs=out_specs, check_vma=False)
```

time: 349 us -> 126 us (0.36); the launches traced: 345 us -> 126 us
  Pallas kernels: 0 us -> 122 us
  other arithmetic: 96.1 us -> 0 us
  waiting for transfers between devices: 84.8 us -> 0 us
  blocking collectives: 65.6 us -> 0 us
  matrix products: 62.3 us -> 0 us
  between operations: 14.9 us -> 0.01 us
  starting transfers between devices: 13.6 us -> 0 us
  local copies, waits for them, and re-layouts: 7.7 us -> 3.79 us
    pallas_call x0 -> x1, Pallas kernels: none -> 122 us  [shards(): pl.pallas_call(kernel, out_shape=jax.ShapeDtypeStruct((NZ, 2 * NY), f32),...]
    psum x1 -> x0, blocking collectives: 65.6 us -> none  [shards(): power = lax.psum(power_local, ('echo', 'plane'))]
    dot_general x12 -> x0, matrix products: 62.3 us -> none  [the longest x4 22 us: along_kz(): jnp.einsum('zw,bwk->bzk', sine, half, preferred_element_type=jnp.float32)]
    psum x2 -> x0, waiting for transfers between devices: 50.2 us -> none  [shards(): total = lax.psum(squares, 'echo')]
    ppermute x4 -> x0, waiting for transfers between devices: 34.5 us -> none  [passed_along(): return lax.ppermute(value, axis, pairs)]
    add x6 -> x0, other arithmetic: 26.5 us -> none  [the longest x2 21.1 us: along_kz(): real_part = first[..., :width] + second[..., width:]]
    another operation x4 -> x0, other arithmetic: 20.1 us -> none
    ppermute x4 -> x0, starting transfers between devices: 13.6 us -> none  [passed_along(): return lax.ppermute(value, axis, pairs)]
  transfers between devices with their start and end apart: 6 -> 0, of which waited for: 3 -> 0; matrix products, arithmetic and copies ran while one was open for 41% -> 0% of each run, Pallas kernels for 0% -> 0%
where the time goes in v1:
time: 126 us
  Pallas kernels  122 us (97%)
  local copies, waits for them, and re-layouts  3.79 us (3%)
    pallas_call x1, Pallas kernels, shards(): pl.pallas_call(kernel, out_shape=jax.ShapeDtypeStruct((NZ, 2 * NY), f32),...  122 us
    unnamed x2, local copies, waits for them, and re-layouts  3.79 us

profile of v1, /device:TPU:32, one launch (start us, length us, event | category | flops | bytes accessed | tf_op | source)
XLA Modules:
  0.0 126.0 jit_solution(7418070378133898952)
XLA Ops:
  0.0 1.5 %copy.12 = s32[1,256,18]{2,1,0:T(8,128)} copy(s32[1,256,18]{1,0,2:T(1,128)} %param.13) | data formatting | bytes 36864 | tf_op args[2]
  1.5 122.2 %solve.1 = f32[256,1024]{1,0:T(8,128)} custom-call(bf16[8,256,1024]{2,1,0:T(8,128)(2,1)} %bitcast.6, bf16[8,256,1024]{2,1,0:T(8,128)(2,1)} %bitcast.7, s32[256,18]{1,0:T(8,128)} %bitcast.9, f32[256,1024]{1,0:T(8,128)} %bitcast.8, bf16[4,256,256]{2,1,0:T(8,128)(2,1)} %constant.14.clone.kf_hbm, bf16[4,256,256]{2,1,0:T(8,128)(2,1)} %constant.15.clone.ki_hbm, ...), custom_call_target="tpu_custom_call" | custom-call | tf_op jit(solution)/shard_map/solve/pallas_call | solution.py:594
  123.6 2.3 %copy.14 = f32[1,1,256,1024]{3,2,1,0:T(8,128)} copy(f32[1,1,256,1024]{3,2,1,0:T(8,128)} %bitcast.5) | data formatting | bytes 2097152

commit v2 on v1

--- a/solution.py
+++ b/solution.py
@@ -22,12 +22,33 @@
 bf16 = jnp.bfloat16
 f32 = jnp.float32
 
-LAG_SEND = 3
-START_PRIMAL = 16
-START_SECOND = 28
-START_COILS = 32
-START_FINAL = 48
-STEPS = START_FINAL + CHUNKS
+HALF = ROWS // 2
+
+AHEAD = 3
+ORDER = ("pow", "us", "sh", "to", "ha", "sq", "coil", "pr")
+STEPS = 96
+PLANS = {
+    "pow": 0xA0,
+    "us": 0x196B6D,
+    "to": 0x2CDA64D46C2982278B000,
+    "ha": 0x15CA8CD23980561B2D80,
+    "sh": 0x43339932AB14C08B94A000,
+    "pr": 0xFFFF000025629927A0000000,
+    "sq": 0x3B2934A95300C5A7360,
+    "coil": 0xF5D540000000244A55BF,
+}
+
+
+SEGMENT = 24
+
+
+def plan_word(stage, segment):
+    plan = PLANS[stage]
+    word = jnp.int32(0)
+    for i in range(-(-STEPS // SEGMENT)):
+        bits = jnp.int32((plan >> (SEGMENT * i)) & (2**SEGMENT - 1))
+        word = jnp.where(segment == i, bits, word)
+    return word
 
 
 def tables(count):
@@ -62,9 +83,10 @@
         lanes[k, (k % 4) * 128 + k // 4] = 1
     lane = np.arange(NY)
     ky = 4 * (lane % 128) + lane // 128
-    where = np.zeros((8, NY), np.int32)
-    where[0] = ky // 30
-    where[1] = ky % 30
+    bits = np.zeros((8, NY), np.int32)
+    bits[0] = ky % 30 % 8
+    spread = np.zeros((128, NY), np.float32)
+    spread[ky % 30 // 8 * 32 + ky // 30, lane] = 1
     cast = lambda a: np.ascontiguousarray(np.stack(a)).astype(ml_dtypes.bfloat16)
     return (
         cast(ky_forward),
@@ -73,7 +95,8 @@
         cast(kz_inverse),
         rows.astype(ml_dtypes.bfloat16),
         lanes.astype(ml_dtypes.bfloat16),
-        where,
+        spread.astype(ml_dtypes.bfloat16),
+        bits,
     )
 
 
@@ -96,8 +119,8 @@
 
 
 def coil_image(c, w, maps, xs):
-    def body(b, _):
-        r = pl.ds(pl.multiple_of(b * 16, 16), 16)
+    for b in range(NZ // 16):
+        r = slice(b * 16, b * 16 + 16)
         xr, xi = [], []
         for t in range(4):
             l = slice(t * 128, (t + 1) * 128)
@@ -112,9 +135,6 @@
         for q, (re, im) in enumerate(outs):
             xs[r, q * 256 : q * 256 + 128] = re.astype(bf16)
             xs[r, q * 256 + 128 : q * 256 + 256] = im.astype(bf16)
-        return 0
-
-    lax.fori_loop(0, NZ // 16, body, 0, unroll=2)
 
 
 def ky_forward(xs, kf, hs):
@@ -157,42 +177,43 @@
         zs[:, q * 256 : (q + 1) * 256] = dot(hp[:, q * 256 : (q + 1) * 256], ki[q])
 
 
-def coil_sum(c, zs, maps, d):
-    def body(b, _):
-        r = pl.ds(pl.multiple_of(b * 16, 16), 16)
-        g = [(zs[r, q * 256 : q * 256 + 128], zs[r, q * 256 + 128 : q * 256 + 256]) for q in range(4)]
-        ar, ai, br, bi = g[0][0] + g[2][0], g[0][1] + g[2][1], g[0][0] - g[2][0], g[0][1] - g[2][1]
-        cr, ci, dr, di = g[1][0] + g[3][0], g[1][1] + g[3][1], g[1][0] - g[3][0], g[1][1] - g[3][1]
-        z = [(ar + cr, ai + ci), (br - di, bi + dr), (ar - cr, ai - ci), (br + di, bi - dr)]
-        for t in range(4):
-            l = slice(t * 128, (t + 1) * 128)
-            h = slice(512 + t * 128, 512 + (t + 1) * 128)
-            mr, mi = maps[c, r, l].astype(f32), maps[c, r, h].astype(f32)
-            zr, zi = z[t]
-            d[r, l] += mr * zr + mi * zi
-            d[r, h] += mr * zi - mi * zr
-        return 0
-
-    lax.fori_loop(0, NZ // 16, body, 0, unroll=2)
-
-
-def build_mask(words, where, mask):
-    column = where[0:1, :]
-    bit = where[1:2, :]
+def coil_sum(coils, zs, maps, d):
+    for b in range(NZ // 16):
+        r = slice(b * 16, b * 16 + 16)
+        sums = [None] * 8
+        for i, c in enumerate(coils):
+            g = [(zs[i, r, q * 256 : q * 256 + 128], zs[i, r, q * 256 + 128 : q * 256 + 256]) for q in range(4)]
+            ar, ai, br, bi = g[0][0] + g[2][0], g[0][1] + g[2][1], g[0][0] - g[2][0], g[0][1] - g[2][1]
+            cr, ci, dr, di = g[1][0] + g[3][0], g[1][1] + g[3][1], g[1][0] - g[3][0], g[1][1] - g[3][1]
+            z = [(ar + cr, ai + ci), (br - di, bi + dr), (ar - cr, ai - ci), (br + di, bi - dr)]
+            for t in range(4):
+                l = slice(t * 128, (t + 1) * 128)
+                h = slice(512 + t * 128, 512 + (t + 1) * 128)
+                mr, mi = maps[c, r, l].astype(f32), maps[c, r, h].astype(f32)
+                zr, zi = z[t]
+                re, im = mr * zr + mi * zi, mr * zi - mi * zr
+                sums[t] = re if i == 0 else sums[t] + re
+                sums[4 + t] = im if i == 0 else sums[4 + t] + im
+        for t in range(8):
+            d[r, t * 128 : (t + 1) * 128] += sums[t]
+
+
+def build_mask(words, turned, spread, bits, mask):
+    wide = jnp.concatenate([words[...].reshape(18, NZ), jnp.zeros((14, NZ), jnp.int32)], 0)
+    turned[...] = jnp.concatenate([jnp.right_shift(wide, 8 * k) & 255 for k in range(4)], 0).T
     for p in range(2):
-        for b in range(8):
-            part = words[pl.ds(p + 32 * b, 16, stride=2), :]
-            spread = jnp.zeros((16, NY), jnp.int32)
-            for w in range(18):
-                spread = jnp.where(column == w, part[:, w : w + 1], spread)
-            value = jnp.right_shift(spread, jnp.broadcast_to(bit, (16, NY))) & 1
-            mask[p, 16 * b : 16 * b + 16, :] = value.astype(f32).astype(bf16)
+        byte = turned[pl.ds(p, 128, stride=2), :].astype(f32).astype(bf16)
+        for n in range(2):
+            l = slice(n * 256, (n + 1) * 256)
+            value = dot(byte, spread[:, l]).astype(jnp.int32)
+            bit = jnp.right_shift(value, jnp.broadcast_to(bits[0:1, l], (128, 256))) & 1
+            mask[p, :, l] = bit.astype(f32).astype(bf16)
 
 
 def kernel(
-    acq_hbm, maps_hbm, words_hbm, u_hbm, kf_hbm, ki_hbm, tf_hbm, ti_hbm, rows_hbm, lanes_hbm, where_hbm,
+    acq_hbm, maps_hbm, words_hbm, u_hbm, kf_hbm, ki_hbm, tf_hbm, ti_hbm, rows_hbm, lanes_hbm, spread_hbm, bits_hbm,
     out_hbm,
-    acq, maps, words, kf, ki, tf, ti, rows, lanes, where,
+    acq, maps, words, turned, kf, ki, tf, ti, rows, lanes, spread, bits,
     acqp, mask, xs, hs, rs, hp, zs,
     cur, extra, w, d, px, pz, py, upb, pxprev,
     n2, crecv, half, xrecv, tot, pw, pw_recv, rad,
@@ -205,12 +226,13 @@
     has_up, has_down = p < 15, p > 0
     partner = (e + 1 - 2 * core, p)
     others_x = [(lax.rem(x + k, 4) * 2 + core, p) for k in (1, 2, 3)]
-    others_y = [(e, z * 4 + lax.rem(y + k, 4)) for k in (1, 2, 3)]
-    others_z = [(e, lax.rem(z + k, 4) * 4 + y) for k in (1, 2, 3)]
+    others_plane = [
+        (e, lax.rem(z + b, 4) * 4 + lax.rem(y + a, 4)) for a in range(4) for b in range(4) if a or b
+    ]
     up, down = (e, p + 1), (e, p - 1)
 
     barrier = pltpu.get_barrier_semaphore()
-    greet = [partner] + others_x + others_y + others_z
+    greet = [partner] + others_x + others_plane
     for device in greet:
         pl.semaphore_signal(barrier, inc=1, device_id=device, device_id_type=MESH)
 
@@ -222,7 +244,7 @@
     def _():
         pl.semaphore_signal(barrier, inc=1, device_id=down, device_id_type=MESH)
 
-    loads = [(u_hbm, cur), (words_hbm, words), (where_hbm, where), (rows_hbm, rows), (lanes_hbm, lanes)]
+    loads = [(u_hbm, cur), (words_hbm, words), (spread_hbm, spread), (bits_hbm, bits), (rows_hbm, rows), (lanes_hbm, lanes)]
     loads += [(kf_hbm, kf), (tf_hbm, tf), (ti_hbm, ti), (ki_hbm, ki)]
     for c in range(COILS):
         loads += [(acq_hbm.at[c], acq.at[c]), (maps_hbm.at[c], maps.at[c])]
@@ -236,6 +258,19 @@
     d[...] = jnp.zeros_like(d)
     extra[NZ : NZ + 8, :] = jnp.zeros((8, 2 * NY), f32)
 
+    copies[0].wait()
+
+    def power_body(b, total):
+        r = pl.ds(pl.multiple_of(b * 8, 8), 8)
+        v = cur[r, :]
+        extra[r, :] = v
+        w[r, :] = v
+        s = v * v
+        for k in range(8):
+            total = total + s[:, k * 128 : (k + 1) * 128]
+        return total
+
+    pw[0] = lax.fori_loop(0, NZ // 8, power_body, jnp.zeros((8, 128), f32), unroll=2)
     pl.semaphore_wait(barrier, len(greet) + has_up.astype(jnp.int32) + has_down.astype(jnp.int32))
 
     def span(c, offset=0):
@@ -263,8 +298,8 @@
             device_id_type=MESH,
         )
 
-    mine = pl.ds(pl.multiple_of(core * 8, 8), 8)
-    theirs = pl.ds(pl.multiple_of(8 - core * 8, 8), 8)
+    mine = pl.ds(pl.multiple_of(core * HALF, 8), HALF)
+    theirs = pl.ds(pl.multiple_of(HALF - core * HALF, 8), HALF)
 
     def send_half(j):
         return pltpu.make_async_remote_copy(
@@ -296,8 +331,8 @@
             device_id_type=MESH,
         )
 
-    power_groups = [[partner], others_x, others_y, others_z]
-    power_first = [0, 1, 4, 7]
+    power_groups = [others_plane, others_x, [partner]]
+    power_first = [0, 15, 18]
 
     def send_power(stage, k):
         slot = power_first[stage] + k
@@ -310,31 +345,11 @@
             device_id_type=MESH,
         )
 
-    @pl.when(has_down)
-    def _():
-        def body(j, _):
-            send_up(j, u_hbm).start()
-            return 0
-
-        lax.fori_loop(0, CHUNKS, body, 0)
-
-    copies[0].wait()
-
-    def power_body(b, total):
-        r = pl.ds(pl.multiple_of(b * 8, 8), 8)
-        v = cur[r, :]
-        extra[r, :] = v
-        w[r, :] = v
-        s = v * v
-        for k in range(8):
-            total = total + s[:, k * 128 : (k + 1) * 128]
-        return total
-
-    pw[0] = lax.fori_loop(0, NZ // 8, power_body, jnp.zeros((8, 128), f32), unroll=2)
-    send_power(0, 0).start()
-    for copy in copies[1:9]:
+    for k in range(15):
+        send_power(0, k).start()
+    for copy in copies[1:10]:
         copy.wait()
-    build_mask(words, where, mask)
+    build_mask(words, turned, spread, bits, mask)
 
     lane = lax.broadcasted_iota(jnp.int32, (ROWS, 2 * NY), 1) & (NY - 1)
     row = lax.broadcasted_iota(jnp.int32, (ROWS, 2 * NY), 0)
@@ -400,6 +415,15 @@
         def _():
             send_dual(j).wait_recv()
 
+        send_half(j).wait_send()
+        for k in range(3):
+            send_x(j, k).wait_send()
+        send_total(j).wait_send()
+
+        @pl.when(has_down)
+        def _():
+            send_up(j, cur).wait_send()
+
         r = span(c)
         below = jnp.where(has_down, pxprev[it, r, :], 0.0)
         wide = pz[pl.ds(pl.multiple_of(c * ROWS, 8), ROWS + 8), :]
@@ -429,113 +453,115 @@
     def store(c):
         return pltpu.make_async_copy(cur.at[span(c)], out_hbm.at[span(c)], out_sem.at[c])
 
-    def coil_first(it, c):
-        @pl.when(it == 0)
-        def _():
-            pltpu.make_async_copy(acq_hbm.at[c], acq.at[c], in_sem.at[9 + 2 * c]).wait()
-            pltpu.make_async_copy(maps_hbm.at[c], maps.at[c], in_sem.at[10 + 2 * c]).wait()
-            permute_acquired(c, acq, acqp, rows, lanes, xs)
-
-        coil_image(c, w, maps, xs)
-        ky_forward(xs, kf, hs)
+    def coil_permute(c):
+        for i in range(2):
+            at = 10 + 2 * (c + i)
+            pltpu.make_async_copy(acq_hbm.at[c + i], acq.at[c + i], in_sem.at[at]).wait()
+            pltpu.make_async_copy(maps_hbm.at[c + i], maps.at[c + i], in_sem.at[at + 1]).wait()
+        for i in range(2):
+            permute_acquired(c + i, acq, acqp, rows, lanes, xs.at[i])
+
+    def coil_first(c):
+        for i in range(2):
+            coil_image(c + i, w, maps, xs.at[i])
+        for i in range(2):
+            ky_forward(xs.at[i], kf, hs.at[i])
 
     def coil_second(c):
-        kz_residual(c, hs, tf, acqp, mask, rs)
-        kz_inverse(rs, ti, hp)
-        ky_inverse(hp, ki, zs)
-        coil_sum(c, zs, maps, d)
-
-    def step(t, _):
-        for stage in range(4):
-
-            @pl.when(t == stage)
+        for i in range(2):
+            kz_residual(c + i, hs.at[i], tf, acqp, mask, rs.at[i])
+        for i in range(2):
+            kz_inverse(rs.at[i], ti, hp.at[i])
+
+    def coil_third(c):
+        for i in range(2):
+            ky_inverse(hp.at[i], ki, zs.at[i])
+        coil_sum([c, c + 1], zs, maps, d)
+
+    def power(stage_now):
+        for stage in range(3):
+
+            @pl.when(jnp.int32(stage_now) == stage)
             def _(stage=stage):
                 total = pw[stage]
                 for k in range(len(power_groups[stage])):
                     send_power(stage, k).wait_recv()
                     total = total + pw_recv[power_first[stage] + k]
-                if stage < 3:
+                if stage < 2:
                     pw[stage + 1] = total
-                    for k in range(3):
+                    for k in range(len(power_groups[stage + 1])):
                         send_power(stage + 1, k).start()
                 else:
                     mean = jnp.sum(total) * (1.0 / 16777216.0) + EPSILON
                     rad[...] = RADIUS_FACTOR * jnp.sqrt(jnp.broadcast_to(mean, (8, 128)))
 
-        first = t - START_SECOND + CHUNKS
-
-        def job(lag):
-            a, b = t - lag, first - lag
-            valid_a = (a >= 0) & (a < CHUNKS)
-            valid_b = (b >= CHUNKS) & (b < JOBS)
-            return valid_a | valid_b, jnp.where(valid_a, a, b)
-
-        def run(lag, work):
-            valid, j = job(lag)
-
-            @pl.when(valid)
-            def _():
-                work(j)
-
-        run(2, totals)
-        run(0, squares)
-        second = t >= START_COILS
-        it = second.astype(jnp.int32)
-        part = t - jnp.where(second, START_COILS, 0)
-
-        @pl.when((part < 2 * COILS) & (lax.rem(part, 2) == 0))
-        def _():
-            coil_first(it, part // 2)
-
-        @pl.when((part < 2 * COILS) & (lax.rem(part, 2) == 1))
-        def _():
-            coil_second(part // 2)
-
-        run(0, halves)
-        run(LAG_SEND, shrink)
-
-        a, b = t - START_PRIMAL, t - START_FINAL
-        valid_a = (a >= 0) & (a < CHUNKS)
-
-        @pl.when(valid_a | (b >= 0))
-        def _():
-            primal(jnp.where(valid_a, a, b + CHUNKS))
-
-        return 0
-
-    lax.fori_loop(0, STEPS, step, 0)
-
-    for stage in range(4):
+    def start_up(j):
+        @pl.when(has_down)
+        def _():
+            send_up(j + AHEAD, cur).start()
+
+    def coil_work(i):
+        early = i < 16
+        s = i - 16
+        c = 2 * jnp.where(early, i // 4, s // 3)
+        part = jnp.where(early, lax.rem(i, 4), lax.rem(s, 3) + 1)
+        for k, work in enumerate((coil_permute, coil_first, coil_second, coil_third)):
+
+            @pl.when(part == k)
+            def _(work=work):
+                work(c)
+
+    works = dict(
+        pow=power, us=start_up, sq=squares, ha=halves, to=totals, sh=shrink, pr=primal, coil=coil_work
+    )
+
+    def segment(n, done):
+        words = [plan_word(stage, n) for stage in ORDER]
+
+        def step(t, done):
+            after = []
+            for stage, word, count in zip(ORDER, words, done):
+                now = jnp.right_shift(word, t) & 1
+
+                @pl.when(now == 1)
+                def _(stage=stage, count=count):
+                    works[stage](count)
+
+                after.append(count + now)
+            return tuple(after)
+
+        return lax.fori_loop(0, SEGMENT, step, done)
+
+    power(0)
+
+    @pl.when(has_down)
+    def _():
+        for j in range(AHEAD):
+            send_up(j, cur).start()
+
+    done = tuple(jnp.int32(int(stage == "pow")) for stage in ORDER)
+    lax.fori_loop(0, -(-STEPS // SEGMENT), segment, done)
+
+    for stage in range(3):
         for k in range(len(power_groups[stage])):
             send_power(stage, k).wait_send()
 
-    def drain(j, _):
-        send_half(j).wait_send()
-        for k in range(3):
-            send_x(j, k).wait_send()
-        send_total(j).wait_send()
-
-        @pl.when(has_down)
-        def _():
-            send_up(j, extra).wait_send()
-
-        @pl.when(has_up & (j >= CHUNKS))
-        def _():
-            send_dual(j).wait_send()
-
-        @pl.when(j < CHUNKS)
-        def _():
-            store(j).wait()
+    def drain(c, _):
+        store(c).wait()
+
+        @pl.when(has_up)
+        def _():
+            send_dual(c + CHUNKS).wait_send()
 
         return 0
 
-    lax.fori_loop(0, JOBS, drain, 0)
+    lax.fori_loop(0, CHUNKS, drain, 0)
 
 
 def shards(acquired, coil_maps, mask_words, start_image):
     acquired = acquired.reshape(COILS, NZ, 2 * NY)
     coil_maps = coil_maps.reshape(COILS, NZ, 2 * NY)
-    words = mask_words.reshape(NZ, 18)
+    words = jnp.transpose(mask_words, (2, 0, 1))
     image = start_image.reshape(NZ, 2 * NY)
     consts = [jnp.asarray(a) for a in constants()]
     anywhere = pl.BlockSpec(memory_space=pl.ANY)
@@ -544,21 +570,23 @@
     scratch = [
         vmem((COILS, NZ, 2 * NY), bf16),
         vmem((COILS, NZ, 2 * NY), bf16),
-        vmem((NZ, 18), jnp.int32),
+        vmem((18, 1, NZ), jnp.int32),
+        vmem((NZ, 128), jnp.int32),
         vmem((4, 256, 256), bf16),
         vmem((4, 256, 256), bf16),
         vmem((2, 256, 256), bf16),
         vmem((2, 256, 256), bf16),
         vmem((256, 256), bf16),
         vmem((512, 512), bf16),
+        vmem((128, NY), bf16),
         vmem((8, NY), jnp.int32),
         vmem((COILS, 2, 256, 512), bf16),
         vmem((2, 128, 512), bf16),
-        vmem((256, 1024), bf16),
-        vmem((2, 256, 512), bf16),
-        vmem((2, 256, 512), bf16),
-        vmem((256, 1024), bf16),
-        vmem((256, 1024)),
+        vmem((2, 256, 1024), bf16),
+        vmem((2, 2, 256, 512), bf16),
+        vmem((2, 2, 256, 512), bf16),
+        vmem((2, 256, 1024), bf16),
+        vmem((2, 256, 1024)),
         vmem((NZ, 2 * NY)),
         vmem((NZ + 8, 2 * NY)),
         vmem((NZ, 2 * NY)),
@@ -569,14 +597,14 @@
         vmem((2, NZ, 2 * NY)),
         vmem((2, NZ, 2 * NY)),
         vmem((JOBS, ROWS, NY)),
-        vmem((JOBS, 8, NY)),
-        vmem((JOBS, 8, NY)),
-        vmem((3, JOBS, 8, NY)),
+        vmem((JOBS, HALF, NY)),
+        vmem((JOBS, HALF, NY)),
+        vmem((3, JOBS, HALF, NY)),
         vmem((JOBS, ROWS, NY)),
-        vmem((4, 8, 128)),
-        vmem((10, 8, 128)),
+        vmem((3, 8, 128)),
+        vmem((19, 8, 128)),
         vmem((8, 128)),
-        dma(9 + 2 * COILS),
+        dma(10 + 2 * COILS),
         dma(JOBS),
         dma(JOBS),
         dma(JOBS),
@@ -587,14 +615,14 @@
         dma(3, JOBS),
         dma(JOBS),
         dma(JOBS),
-        dma(10),
-        dma(10),
+        dma(19),
+        dma(19),
         dma(CHUNKS),
     ]
     solved = pl.pallas_call(
         kernel,
         out_shape=jax.ShapeDtypeStruct((NZ, 2 * NY), f32),
-        in_specs=[anywhere] * 11,
+        in_specs=[anywhere] * 12,
         out_specs=anywhere,
         scratch_shapes=scratch,
         compiler_params=pltpu.CompilerParams(

time: 126 us -> 79.7 us (0.63)
  Pallas kernels: 122 us -> 77.2 us
  local copies, waits for them, and re-layouts: 3.79 us -> 2.31 us
    pallas_call x1, Pallas kernels: 122 us -> 77.2 us  [shards(): pl.pallas_call(kernel, out_shape=jax.ShapeDtypeStruct((NZ, 2 * NY), f32),...]
    unnamed x2 -> x1, local copies, waits for them, and re-layouts: 3.79 us -> 2.31 us
where the time goes in v2:
time: 79.7 us; the launch traced here: 79.5 us
  Pallas kernels  77.2 us (97%)
  local copies, waits for them, and re-layouts  2.31 us (3%)
    pallas_call x1, Pallas kernels, shards(): pl.pallas_call(kernel, out_shape=jax.ShapeDtypeStruct((NZ, 2 * NY), f32),...  77.2 us
    unnamed x1, local copies, waits for them, and re-layouts  2.31 us

profile of v2, /device:TPU:32, one launch (start us, length us, event | category | flops | bytes accessed | tf_op | source)
XLA Modules:
  0.0 79.5 jit_solution(8956427495599353500)
XLA Ops:
  0.0 77.2 %solve.1 = f32[256,1024]{1,0:T(8,128)} custom-call(bf16[8,256,1024]{2,1,0:T(8,128)(2,1)} %bitcast.5, bf16[8,256,1024]{2,1,0:T(8,128)(2,1)} %bitcast.6, s32[18,1,256]{2,1,0:T(1,128)} %bitcast.9, f32[256,1024]{1,0:T(8,128)} %bitcast.8, bf16[4,256,256]{2,1,0:T(8,128)(2,1)} %constant.16.clone.kf_hbm, bf16[4,256,256]{2,1,0:T(8,128)(2,1)} %constant.17.clone.ki_hbm, ...), custom_call_target="tpu_custom_call" | custom-call | tf_op jit(solution)/shard_map/solve/pallas_call | solution.py:622
  77.2 2.3 %copy.14 = f32[1,1,256,1024]{3,2,1,0:T(8,128)} copy(f32[1,1,256,1024]{3,2,1,0:T(8,128)} %bitcast.7) | data formatting | bytes 2097152

commit v3 on v2

--- a/solution.py
+++ b/solution.py
@@ -15,7 +15,7 @@
 COILS = 8
 RADIUS_FACTOR = 0.5
 EPSILON = 1e-06
-ROWS = 16
+ROWS = 32
 CHUNKS = NZ // ROWS
 JOBS = 2 * CHUNKS
 MESH = pl.DeviceIdType.MESH
@@ -24,18 +24,20 @@
 
 HALF = ROWS // 2
 
-AHEAD = 3
-ORDER = ("pow", "us", "sh", "to", "ha", "sq", "coil", "pr")
-STEPS = 96
+BEFORE = 1
+AHEAD = 2
+ORDER = ("pow", "us", "sq", "to", "pr", "ha", "coil", "sh", "fin")
+STEPS = 50
 PLANS = {
-    "pow": 0xA0,
-    "us": 0x196B6D,
-    "to": 0x2CDA64D46C2982278B000,
-    "ha": 0x15CA8CD23980561B2D80,
-    "sh": 0x43339932AB14C08B94A000,
-    "pr": 0xFFFF000025629927A0000000,
-    "sq": 0x3B2934A95300C5A7360,
-    "coil": 0xF5D540000000244A55BF,
+    "pow": 0x60,
+    "us": 0xA53,
+    "to": 0x2A8B9E91040,
+    "ha": 0x2A5CE92504,
+    "sh": 0x4A93AF24080,
+    "pr": 0x384AA3AF00000,
+    "sq": 0x153AE24A42,
+    "coil": 0x3FF600D9FFE,
+    "fin": 0x3FC0000000000,
 }
 
 
@@ -347,6 +349,11 @@
 
     for k in range(15):
         send_power(0, k).start()
+    @pl.when(has_down)
+    def _():
+        for j in range(BEFORE):
+            send_up(j, cur).start()
+
     for copy in copies[1:10]:
         copy.wait()
     build_mask(words, turned, spread, bits, mask)
@@ -430,14 +437,14 @@
         vy = py[r, :]
         before = jnp.where(lane > 0, pltpu.roll(vy, 1, 1), 0.0)
         g = (below - px[r, :]) + (wide[7 : ROWS + 7] - wide[8:]) + (before - vy)
-        factor = jnp.where(it == 0, 0.2, 0.36).astype(f32)
         old = cur[r, :]
-        new = old - 0.25 * (factor * d[r, :] + g)
-        cur[r, :] = new
+        new = old - 0.25 * g
 
         @pl.when(it == 0)
         def _():
-            ahead = 2.0 * new - old
+            first = new - 0.05 * d[r, :]
+            ahead = 2.0 * first - old
+            cur[r, :] = first
             extra[r, :] = ahead
             w[r, :] = (0.2 / 0.36) * ahead + (0.16 / 0.36) * old
             d[r, :] = jnp.zeros((ROWS, 2 * NY), f32)
@@ -448,7 +455,12 @@
 
         @pl.when(it == 1)
         def _():
-            store(c).start()
+            cur[r, :] = new
+
+    def finish(c):
+        r = span(c)
+        cur[r, :] = cur[r, :] - 0.09 * d[r, :]
+        store(c).start()
 
     def store(c):
         return pltpu.make_async_copy(cur.at[span(c)], out_hbm.at[span(c)], out_sem.at[c])
@@ -512,7 +524,7 @@
                 work(c)
 
     works = dict(
-        pow=power, us=start_up, sq=squares, ha=halves, to=totals, sh=shrink, pr=primal, coil=coil_work
+        pow=power, us=start_up, sq=squares, ha=halves, to=totals, sh=shrink, pr=primal, fin=finish, coil=coil_work
     )
 
     def segment(n, done):
@@ -536,7 +548,7 @@
 
     @pl.when(has_down)
     def _():
-        for j in range(AHEAD):
+        for j in range(BEFORE, AHEAD):
             send_up(j, cur).start()
 
     done = tuple(jnp.int32(int(stage == "pow")) for stage in ORDER)

time: 79.7 us -> 78.4 us (0.984)
  Pallas kernels: 77.2 us -> 75.9 us
    pallas_call x1, Pallas kernels: 77.2 us -> 75.9 us  [shards(): pl.pallas_call(kernel, out_shape=jax.ShapeDtypeStruct((NZ, 2 * NY), f32),...]
where the time goes in v3:
time: 78.4 us; the launch traced here: 78.2 us
  Pallas kernels  75.9 us (97%)
  local copies, waits for them, and re-layouts  2.31 us (3%)
    pallas_call x1, Pallas kernels, shards(): pl.pallas_call(kernel, out_shape=jax.ShapeDtypeStruct((NZ, 2 * NY), f32),...  75.9 us
    unnamed x1, local copies, waits for them, and re-layouts  2.31 us

profile of v3, /device:TPU:32, one launch (start us, length us, event | category | flops | bytes accessed | tf_op | source)
XLA Modules:
  0.0 78.2 jit_solution(6807705306934118435)
XLA Ops:
  0.0 75.9 %solve.1 = f32[256,1024]{1,0:T(8,128)} custom-call(bf16[8,256,1024]{2,1,0:T(8,128)(2,1)} %bitcast.5, bf16[8,256,1024]{2,1,0:T(8,128)(2,1)} %bitcast.6, s32[18,1,256]{2,1,0:T(1,128)} %bitcast.9, f32[256,1024]{1,0:T(8,128)} %bitcast.8, bf16[4,256,256]{2,1,0:T(8,128)(2,1)} %constant.16.clone.kf_hbm, bf16[4,256,256]{2,1,0:T(8,128)(2,1)} %constant.17.clone.ki_hbm, ...), custom_call_target="tpu_custom_call" | custom-call | tf_op jit(solution)/shard_map/solve/pallas_call | solution.py:634
  75.9 2.3 %copy.14 = f32[1,1,256,1024]{3,2,1,0:T(8,128)} copy(f32[1,1,256,1024]{3,2,1,0:T(8,128)} %bitcast.7) | data formatting | bytes 2097152

commit v4 on v3

--- a/solution.py
+++ b/solution.py
@@ -25,19 +25,19 @@
 HALF = ROWS // 2
 
 BEFORE = 1
-AHEAD = 2
-ORDER = ("pow", "us", "sq", "to", "pr", "ha", "coil", "sh", "fin")
-STEPS = 50
+AHEAD = 3
+ORDER = ("pow", "us", "sh", "to", "sq", "pr", "ha", "coil", "fin")
+STEPS = 53
 PLANS = {
-    "pow": 0x60,
-    "us": 0xA53,
-    "to": 0x2A8B9E91040,
-    "ha": 0x2A5CE92504,
-    "sh": 0x4A93AF24080,
-    "pr": 0x384AA3AF00000,
-    "sq": 0x153AE24A42,
-    "coil": 0x3FF600D9FFE,
-    "fin": 0x3FC0000000000,
+    "pow": 0x140,
+    "us": 0x893,
+    "to": 0x8A8B4B918400,
+    "ha": 0x4A555649220,
+    "sh": 0x4252697451000,
+    "pr": 0x1C92934B600000,
+    "sq": 0x24AAAC92888,
+    "coil": 0x3FEE0013F9FE,
+    "fin": 0x1FE00000000000,
 }
 
 

time: 78.4 us -> 77.9 us (level)
  no operation moved by 1% of the time
where the time goes in v4:
time: 77.9 us; the launch traced here: 77.7 us
  Pallas kernels  75.4 us (97%)
  local copies, waits for them, and re-layouts  2.31 us (3%)
    pallas_call x1, Pallas kernels, shards(): pl.pallas_call(kernel, out_shape=jax.ShapeDtypeStruct((NZ, 2 * NY), f32),...  75.4 us
    unnamed x1, local copies, waits for them, and re-layouts  2.31 us

profile of v4, /device:TPU:32, one launch (start us, length us, event | category | flops | bytes accessed | tf_op | source)
XLA Modules:
  0.0 77.7 jit_solution(6722359117003236286)
XLA Ops:
  0.0 75.4 %solve.1 = f32[256,1024]{1,0:T(8,128)} custom-call(bf16[8,256,1024]{2,1,0:T(8,128)(2,1)} %bitcast.5, bf16[8,256,1024]{2,1,0:T(8,128)(2,1)} %bitcast.6, s32[18,1,256]{2,1,0:T(1,128)} %bitcast.9, f32[256,1024]{1,0:T(8,128)} %bitcast.8, bf16[4,256,256]{2,1,0:T(8,128)(2,1)} %constant.16.clone.kf_hbm, bf16[4,256,256]{2,1,0:T(8,128)(2,1)} %constant.17.clone.ki_hbm, ...), custom_call_target="tpu_custom_call" | custom-call | tf_op jit(solution)/shard_map/solve/pallas_call | solution.py:634
  75.4 2.3 %copy.14 = f32[1,1,256,1024]{3,2,1,0:T(8,128)} copy(f32[1,1,256,1024]{3,2,1,0:T(8,128)} %bitcast.7) | data formatting | bytes 2097152
